TPU v7x, 32 devices: a whole 2x2x4 slice. The times are simulated.
32 devices in a mesh: gen: 8 (over z, x), split: 4 (over y, core).
Axes of the slice: x: 2, y: 2, z: 4, core: 2. Of those that a mesh axis runs over, the one named last changes fastest.
Arguments:
- hidden: bfloat16 [32, 256, 8192], P(None, 'gen', 'split'), may hold values from -12 to 12
- w_proj: bfloat16 [8192, 1024], P('split', 'gen'), may hold values from -0.0625 to 0.0625
- slot_prompt: int32 [256], P('gen'), may hold values from 0 to 7, as said below
- lengths: int32 [256], P('gen'), may hold values from 1 to 32
- weights: bfloat16 [256], P('gen'), may hold values from 0.099609375 to 10
- owner: int32 [8], replicated, may hold values from 0 to 7, each once
Outputs:
- utility: float32 [8, 64], P('gen')
Inputs may be any that keep to these rules, and one draw needn't show every extreme that they name: `slot_prompt`: each prompt names 1 to 64 slots and one prompt names exactly 64; each generator device (a run of 32 slots) holds at most 8 slots of one prompt, and some device holds exactly 8. `owner`: each index along gen owns exactly one prompt.
All inputs are finite; a program needn't handle non-finite values.
Results may differ from a plain program's by a relative error of at most 0.0015.
Values may be sent and summed in bfloat16 or wider, within the bound.
A program may use at most 64 MiB of HBM per device.

v0:
```python
import math

import jax
import jax.numpy as jnp
from jax import lax
from jax.sharding import PartitionSpec as P

MAXS = 64


def column_best(row_flat, gathered, member_len):
    amount = gathered.shape[0]
    slots_here = gathered.shape[1]
    col_flat = gathered.reshape(amount * slots_here, gathered.shape[2])
    scores = lax.dot_general(
        row_flat, col_flat, (((1,), (1,)), ((), ())), preferred_element_type=jnp.float32
    )
    scores = scores.reshape(row_flat.shape[0] // slots_here, slots_here, amount, slots_here)
    positions = jnp.arange(amount, dtype=jnp.int32)
    col_ok = positions[:, None] < member_len[None, :]
    scores = jnp.where(col_ok[None, None, :, :], scores, jnp.float32(-2.0))
    return jnp.max(scores, axis=2)


def body(hidden, w_proj, slot_prompt, lengths, weights, owner):
    n_gen = lax.axis_size("gen")
    n_split = lax.axis_size("split")
    seq_part = hidden.shape[0] // n_split
    slots = hidden.shape[1]
    w_block = lax.all_gather(w_proj, "gen", axis=1, tiled=True)
    emb_width = w_block.shape[1]
    projected = lax.psum_scatter(
        jnp.einsum("psh,he->pse", hidden, w_block, preferred_element_type=jnp.float32).astype(
            jnp.bfloat16
        ),
        "split",
        scatter_dimension=0,
        tiled=True,
    ).astype(jnp.float32)
    scale = lax.rsqrt(jnp.mean(projected * projected, axis=-1, keepdims=True) + 1e-06) / math.sqrt(
        emb_width
    )
    unit = (projected * scale).astype(jnp.bfloat16)
    owner_cap = (MAXS + n_gen - 1) // n_gen
    buffer_slots = n_gen * owner_cap
    owner_hit = slot_prompt[:, None] == jnp.arange(n_gen, dtype=jnp.int32)[None, :]
    dest_owner = jnp.sum(jnp.where(owner_hit, owner[None, :], 0), axis=1)
    local_index = jnp.arange(slots, dtype=jnp.int32)
    same_prompt = slot_prompt[:, None] == slot_prompt[None, :]
    earlier = local_index[:, None] > local_index[None, :]
    rank = jnp.sum((same_prompt & earlier).astype(jnp.int32), axis=1)
    destination = dest_owner * owner_cap + rank
    matches = destination[None, :] == jnp.arange(buffer_slots, dtype=jnp.int32)[:, None]
    occupied = jnp.sum(matches.astype(jnp.int32), axis=1) > 0
    source_slot = jnp.sum(jnp.where(matches, local_index[None, :], 0), axis=1)
    send_unit = jnp.take(unit, source_slot, axis=1)
    send_len = jnp.where(occupied, jnp.take(lengths, source_slot), 0).astype(jnp.bfloat16)
    send_weight = jnp.where(occupied, jnp.take(weights, source_slot), jnp.zeros((), jnp.bfloat16))
    send_meta = jnp.stack([send_len, send_weight], axis=0)
    arrived, arrived_meta = (
        lax.all_to_all(send_unit, "gen", split_axis=1, concat_axis=1, tiled=True),
        lax.all_to_all(send_meta, "gen", split_axis=1, concat_axis=1, tiled=True),
    )
    arrived_len = arrived_meta[0].astype(jnp.int32)
    arrived_weight = arrived_meta[1].astype(jnp.float32)
    running = jnp.cumsum((arrived_len > 0).astype(jnp.int32))
    targets = jnp.arange(MAXS, dtype=jnp.int32)
    position = jnp.sum((running[None, :] <= targets[:, None]).astype(jnp.int32), axis=1)
    position = jnp.minimum(position, buffer_slots - 1)
    filled = targets < running[-1]
    member_len = jnp.where(filled, jnp.take(arrived_len, position), 0)
    member_weight = jnp.where(filled, jnp.take(arrived_weight, position), jnp.float32(0.0))
    mine = jnp.take(arrived, position, axis=1)
    row_flat = mine.reshape(seq_part * MAXS, emb_width)
    every = lax.all_gather(arrived, "split", axis=0, tiled=True)
    columns = jnp.take(every, position, axis=1)
    best = column_best(row_flat, columns, member_len)
    my_positions = lax.axis_index("split") * seq_part + jnp.arange(seq_part, dtype=jnp.int32)
    row_ok = my_positions[:, None] < member_len[None, :]
    partial_sums = jnp.sum(jnp.where(row_ok[:, :, None], best, jnp.float32(0.0)), axis=0)
    summed = lax.psum(partial_sums, "split")
    recall = summed / jnp.maximum(member_len, 1).astype(jnp.float32)[:, None]
    score = 0.5 * (recall + recall.T)
    util = jnp.sum(score * member_weight[None, :], axis=1) / jnp.sum(member_weight)
    util = jnp.where(filled, util, jnp.float32(0.0))
    return util[None, :]


def solution(mesh):
    placed = (P(None, "gen", "split"), P("split", "gen"), P("gen"), P("gen"), P("gen"), P())
    return jax.shard_map(
        body, mesh=mesh, in_specs=placed, out_specs=P("gen", None), check_vma=False
    )
```

profile of v0, /device:TPU:29, one launch (start us, length us, event | category | flops | bytes accessed | tf_op | source)
XLA Modules:
  0.0 226.3 jit_solution(9306357788528423125)
XLA Ops:
  6.5 0.7 all-gather.3.cloned.1.call-update
  7.3 0.0 reduce-scatter.2.cloned.1.call-start
  7.3 76.3 %all-gather.3.cloned.1.call-done = bf16[2048,1024]{1,0:T(8,128)(2,1)} async-done(((bf16[2048,128]{1,0:T(8,128)(2,1)}), bf16[2048,1024]{1,0:T(8,128)(2,1)}) %all-gather.3.cloned.1.call-update) | async-done | bytes 4194320 | tf_op jit(solution)/shard_map/all_gather | solution.py:30
  83.7 9.3 %fusion.7 = bf16[32,32,1024]{2,1,0:T(8,128)(2,1)} fusion(bf16[32,32,2048]{2,1,0:T(8,128)(2,1)} %param.6, bf16[2048,1024]{1,0:T(8,128)(2,1)} %all-gather.3.cloned.1.call-done), kind=kOutput, calls=%fused_computation.14 | convolution fusion | flops 4296015872 | bytes 10485760 | tf_op jit(solution)/shard_map/psh,he->pse/dot_general | solution.py:33
  93.0 0.0 all-gather.5.cloned.1.call-start
  93.0 0.2 convert_reduce_fusion.2
  93.2 0.1 select_reduce_fusion.3
  93.3 0.1 select_reduce_fusion.2
  93.4 30.2 %reduce-scatter.2.cloned.1.call-done = bf16[8,32,1024]{2,1,0:T(8,128)(2,1)} async-done(((bf16[32,32,1024]{2,1,0:T(8,128)(2,1)}), bf16[8,32,1024]{2,1,0:T(8,128)(2,1)}) %reduce-scatter.2.cloned.1.call-update) | async-done | bytes 524304 | tf_op jit(solution)/shard_map/reduce_scatter | solution.py:32
  123.6 1.2 fusion.10
  124.8 1.2 fusion.11
  126.0 0.3 copy.24
  126.4 0.6 gather_fusion.3
  127.0 0.2 select_bitcast_fusion.2
  127.1 28.5 %all_to_all.11 = bf16[8,64,1024]{2,0,1:T(8,128)(2,1)} all-to-all(bf16[8,64,1024]{2,0,1:T(8,128)(2,1)S(1)} %select_bitcast_fusion.2), channel_id=1, replica_groups=mesh['gen'=8,'split'=4] {'gen'}, dimensions={1} | all-to-all | bytes 2097152 | tf_op jit(solution)/shard_map/all_to_all | solution.py:61
  155.7 0.1 reduce_sum.89
  155.7 0.8 gather_fusion
  156.5 0.1 gather.33
  156.6 0.1 gt.47
  156.7 0.8 gather_fusion.1
  157.5 0.1 gather.35
  157.6 0.6 copy.21
  158.2 5.8 %all-to-all-start = ((bf16[2,8,8]{2,0,1:T(2,128)(2,1)}), bf16[2,8,8]{2,0,1:T(2,128)(2,1)S(1)}, u32[]{:S(2)}, u32[]{:S(2)}) async-start(bf16[2,8,8]{2,0,1:T(2,128)(2,1)} %copy.21), calls=%async_computation | async-start | bytes 8192 | tf_op jit(solution)/shard_map/all_to_all | solution.py:62
  164.1 2.3 %all-to-all-done = bf16[2,8,8]{2,0,1:T(2,128)(2,1)S(1)} async-done(((bf16[2,8,8]{2,0,1:T(2,128)(2,1)}), bf16[2,8,8]{2,0,1:T(2,128)(2,1)S(1)}, u32[]{:S(2)}, u32[]{:S(2)}) %all-to-all-start) | async-done | bytes 288 | tf_op jit(solution)/shard_map/all_to_all | solution.py:62
  166.4 0.1 reshape.393
  166.5 0.1 reduce-window.4
  166.6 0.1 reduce
  166.7 0.5 slice.30
  167.2 0.1 reshape.333
  167.3 0.1 reshape.332
  167.4 0.1 convert_reduce_fusion
  167.5 0.8 gather_fusion.6
  168.3 0.8 gather_fusion.2
  169.1 1.2 fusion.19
  170.3 0.6 maximum_convert_fusion
  170.8 0.1 broadcast_compare_fusion
  170.9 1.8 gather_fusion.4
  172.8 0.2 select_bitcast_fusion.1
  172.9 18.5 %all-gather.5.cloned.1.call-done = bf16[32,64,1024]{2,0,1:T(8,128)(2,1)} async-done(((bf16[8,64,1024]{2,0,1:T(8,128)(2,1)}), bf16[32,64,1024]{2,0,1:T(8,128)(2,1)}) %all-gather.5.cloned.1.call-update) | async-done | bytes 4194320 | tf_op jit(solution)/shard_map/all_gather | solution.py:75
  191.5 5.0 %gather_fusion.5 = bf16[64,32,1024]{2,1,0:T(8,128)(2,1)} fusion(bf16[32,64,1024]{2,0,1:T(8,128)(2,1)} %all-gather.5.cloned.1.call-done, s32[1024]{0:T(1024)S(1)} %pad_clamp_fusion), kind=kCustom, calls=%fused_computation.5 | custom fusion | bytes 8388864 | tf_op jit(solution)/shard_map/jit(_take)/gather | solution.py:76
  196.4 2.6 %select_bitcast_fusion = bf16[32,64,1024]{2,0,1:T(8,128)(2,1)S(1)} fusion(bf16[64,32,1024]{2,1,0:T(8,128)(2,1)} %gather_fusion.5, pred[64]{0:T(512)(128)(4,1)S(1)} %get-tuple-element.9), kind=kLoop, calls=%fused_computation.13 | loop fusion | flops 2097152 | bytes 8388672 | tf_op jit(solution)/shard_map/jit(_take)/select_n | solution.py:76
  199.1 8.3 %select_reduce_fusion = f32[8,64,64]{2,1,0:T(8,128)S(1)} fusion(pred[32,64]{1,0:T(8,128)(4,1)S(1)} %iota_compare_fusion.1, bf16[32,64,1024]{2,0,1:T(8,128)(2,1)S(1)} %select_bitcast_fusion, bf16[8,64,1024,1]{2,0,1,3:T(8,128)(2,1)S(1)} %select_bitcast_fusion.1), kind=kOutput, calls=%fused_computation.7 | convolution fusion | flops 2149548032 | bytes 5376000 | tf_op jit(solution)/shard_map/dot_general | solution.py:15
  207.4 0.1 select_reduce_fusion.1
  207.5 10.2 %psum.7 = f32[64,64]{1,0:T(8,128)S(1)} all-reduce(f32[64,64]{1,0:T(8,128)S(1)} %select_reduce_fusion.1), channel_id=1, replica_groups=mesh['gen'=8,'split'=4] {'split'}, use_global_device_ids=true, to_apply=%region_10.11 | all-reduce | flops 4096 | bytes 32768 | tf_op jit(solution)/shard_map/psum | solution.py:81
  217.7 0.1 broadcast_divide_fusion
  217.8 0.1 copy.27
  217.9 0.2 fusion.14
  218.1 1.7 compare_select_fusion.5
  (28 shorter events, 0.2 us)
Async XLA Ops:
  6.5 149.2 %copy-start = (s32[32]{0:T(128)S(1)}, s32[32]{0:T(128)}, u32[]{:S(2)}) copy-start(s32[32]{0:T(128)} %param.9) | copy-start | bytes 388
  6.5 77.1 %all-gather.3.cloned.1.call-start = ((), (), s32[]{:S(2)}) async-start(), calls=%async_computation.3 | async-start | bytes 4718592 | tf_op jit(solution)/shard_map/all_gather | solution.py:30
  7.3 85.8 %copy-start.2 = (s32[32]{0:T(128)S(1)}, s32[32]{0:T(128)}, u32[]{:S(2)}) copy-start(s32[32]{0:T(128)} %param.8) | copy-start | bytes 388
  7.3 86.0 %copy-start.3 = (s32[8]{0:T(128)S(1)}, s32[8]{0:T(128)}, u32[]{:S(2)}) copy-start(s32[8]{0:T(128)} %param.11) | copy-start | bytes 100
  7.3 116.3 %reduce-scatter.2.cloned.1.call-start = ((), (), s32[]{:S(2)}) async-start(), calls=%async_computation.4 | async-start | bytes 2621440 | tf_op jit(solution)/shard_map/reduce_scatter | solution.py:32
  93.0 98.5 %all-gather.5.cloned.1.call-start = ((), (), s32[]{:S(2)}) async-start(), calls=%async_computation.5 | async-start | bytes 5242880 | tf_op jit(solution)/shard_map/all_gather | solution.py:75
  126.3 30.4 %copy-start.1 = (bf16[32]{0:T(256)(128)(2,1)S(1)}, bf16[32]{0:T(256)(128)(2,1)}, u32[]{:S(2)}) copy-start(bf16[32]{0:T(256)(128)(2,1)} %param.10) | copy-start | bytes 196
  158.2 8.2 %all-to-all-start = ((bf16[2,8,8]{2,0,1:T(2,128)(2,1)}), bf16[2,8,8]{2,0,1:T(2,128)(2,1)S(1)}, u32[]{:S(2)}, u32[]{:S(2)}) async-start(bf16[2,8,8]{2,0,1:T(2,128)(2,1)} %copy.21), calls=%async_computation | async-start | bytes 8192 | tf_op jit(solution)/shard_map/all_to_all | solution.py:62
Sparse Core Ops, SparseCore 0:
  9.4 74.2 all-gather.2
  93.1 30.4 reduce-scatter.1
  155.8 35.6 all-gather.4
where the time goes:
time: 229 us; the launch traced here: 226 us
  waiting for transfers between devices  128 us (56%)
  blocking collectives  38.7 us (17%)
  matrix products  17.6 us (8%)
  between operations  13.3 us (6%)
  local copies, waits for them, and re-layouts  12.6 us (6%)
  other arithmetic  10.1 us (4%)
  starting transfers between devices  5.92 us (3%)
    all_gather x1, waiting for transfers between devices, body(): w_block = lax.all_gather(w_proj, 'gen', axis=1, tiled=True)  76.3 us
    reduce_scatter x1, waiting for transfers between devices, body(): lax.psum_scatter(jnp.einsum('psh,he->pse', hidden, w_block, preferred_ele...  30.2 us
    all_to_all x1, blocking collectives, body(): lax.all_to_all(send_unit, 'gen', split_axis=1, concat_axis=1, tiled=True)  28.5 us
    all_gather x1, waiting for transfers between devices, body(): every = lax.all_gather(arrived, 'split', axis=0, tiled=True)  18.5 us
    psum x1, blocking collectives, body(): summed = lax.psum(partial_sums, 'split')  10.2 us
    dot_general x1, matrix products, body(): jnp.einsum('psh,he->pse', hidden, w_block, preferred_element_type=jnp.flo...  9.28 us
    dot_general x1, matrix products, column_best(): lax.dot_general(row_flat, col_flat, (((1,), (1,)), ((), ())), preferred_e...  8.3 us
    all_to_all x1, starting transfers between devices, body(): lax.all_to_all(send_meta, 'gen', split_axis=1, concat_axis=1, tiled=True)  5.84 us
  transfers between devices with their start and end apart: 4, of which 4 were waited for; matrix products, arithmetic and copies ran while one was open for 4% of the time, Pallas kernels for 0%

commit v1 on v0

--- a/solution.py
+++ b/solution.py
@@ -1,11 +1,229 @@
+import functools
 import math
 
 import jax
 import jax.numpy as jnp
 from jax import lax
+from jax.experimental import pallas as pl
+from jax.experimental.pallas import tpu as pltpu
 from jax.sharding import PartitionSpec as P
 
 MAXS = 64
+PAIR = 2
+MESH = pl.DeviceIdType.MESH
+
+
+def greet(n_gen, n_split):
+    g = lax.axis_index("gen")
+    s = lax.axis_index("split")
+    barrier = pltpu.get_barrier_semaphore()
+    for i in range(1, n_gen):
+        pl.semaphore_signal(
+            barrier, inc=1, device_id={"gen": lax.rem(g + i, n_gen)}, device_id_type=MESH
+        )
+    for i in range(1, n_split):
+        pl.semaphore_signal(
+            barrier, inc=1, device_id={"split": lax.rem(s + i, n_split)}, device_id_type=MESH
+        )
+    pl.semaphore_wait(barrier, n_gen + n_split - 2)
+
+
+def project_kernel(
+    n_gen, n_split, h_ref, w_ref, meta_ref, unit_ref, metas_ref,
+    h_held, w_held, term, inbox, h_sem, up_sem, down_sem, side_sem, line_sem, cross_sem,
+    out_sem, in_sem, meta_send, meta_recv,
+):
+    g = lax.axis_index("gen")
+    s = lax.axis_index("split")
+    n_line = n_gen // PAIR
+    z, x = g // PAIR, lax.rem(g, PAIR)
+    width = w_ref.shape[1]
+    rows = h_held.shape[0] // n_split
+    load = pltpu.make_async_copy(h_ref, h_held, h_sem)
+    load.start()
+    greet(n_gen, n_split)
+
+    def shard(line, side):
+        return w_held.at[line, :, pl.ds(pl.multiple_of(side * width, width), width)]
+
+    def move(source, line, line_to, side_to, send_sem, recv_sem):
+        return pltpu.make_async_remote_copy(
+            src_ref=source, dst_ref=shard(line, x), send_sem=send_sem, recv_sem=recv_sem,
+            device_id={"gen": line_to * PAIR + side_to}, device_id_type=MESH,
+        )
+
+    def up(source, line):
+        return move(source, line, z + 1, x, up_sem.at[line], line_sem.at[line])
+
+    def down(source, line):
+        return move(source, line, z - 1, x, down_sem.at[line], line_sem.at[line])
+
+    def side(source, line):
+        return move(source, line, z, 1 - x, side_sem.at[line], cross_sem.at[line])
+
+    def meta_copy(i):
+        peer = lax.rem(g + i, n_gen)
+        return pltpu.make_async_remote_copy(
+            src_ref=meta_ref, dst_ref=metas_ref.at[g], send_sem=meta_send.at[peer],
+            recv_sem=meta_recv.at[g], device_id={"gen": peer}, device_id_type=MESH,
+        )
+
+    def landed(ref, sem):
+        pltpu.make_async_copy(ref, ref, sem).wait()
+
+    side(w_ref, z).start()
+
+    @pl.when(z < n_line - 1)
+    def _():
+        up(w_ref, z).start()
+
+    @pl.when(z > 0)
+    def _():
+        down(w_ref, z).start()
+
+    for i in range(1, n_gen):
+        meta_copy(i).start()
+    metas_ref[g] = meta_ref[...]
+    w_held[z, :, pl.ds(pl.multiple_of(x * width, width), width)] = w_ref[...]
+    load.wait()
+
+    def term_copy(line, peer):
+        return pltpu.make_async_remote_copy(
+            src_ref=term.at[line, peer], dst_ref=inbox.at[line, s], send_sem=out_sem.at[line, peer],
+            recv_sem=in_sem.at[line, s], device_id={"split": peer}, device_id_type=MESH,
+        )
+
+    def product(line, part):
+        start = pl.multiple_of(part * rows, rows)
+        return jnp.dot(
+            h_held[pl.ds(start, rows), :], w_held[line], preferred_element_type=jnp.float32
+        ).astype(jnp.bfloat16)
+
+    def group(line):
+        landed(shard(line, 1 - x), cross_sem.at[line])
+
+        def step(i, carry):
+            peer = lax.rem(s + i, n_split)
+            term[line, peer] = product(line, peer)
+            term_copy(line, peer).start()
+            return carry
+
+        lax.fori_loop(1, n_split, step, 0)
+        inbox[line, s] = product(line, s)
+
+    def group_at(distance):
+        if distance == 0:
+            group(z)
+            return
+
+        @pl.when(z - distance >= 0)
+        def _():
+            group(z - distance)
+
+        @pl.when(z + distance < n_line)
+        def _():
+            group(z + distance)
+
+    for distance in range(1, n_line):
+
+        @pl.when(z - distance >= 0)
+        def _():
+            line = z - distance
+            landed(shard(line, x), line_sem.at[line])
+
+            @pl.when(z < n_line - 1)
+            def _():
+                up(shard(line, x), line).start()
+
+            side(shard(line, x), line).start()
+
+        @pl.when(z + distance < n_line)
+        def _():
+            line = z + distance
+            landed(shard(line, x), line_sem.at[line])
+
+            @pl.when(z > 0)
+            def _():
+                down(shard(line, x), line).start()
+
+            side(shard(line, x), line).start()
+
+        group_at(distance - 1)
+    group_at(n_line - 1)
+
+    for line in range(n_line):
+        for i in range(1, n_split):
+            peer = lax.rem(s + i, n_split)
+            landed(inbox.at[line, peer], in_sem.at[line, peer])
+    chunk = 64
+    full = unit_ref.shape[1]
+    wide = PAIR * width
+
+    @pl.loop(0, rows // chunk)
+    def _(c):
+        here = pl.ds(pl.multiple_of(c * chunk, chunk), chunk)
+        squares = jnp.zeros((chunk, 1), jnp.float32)
+        sums = []
+        for line in range(n_line):
+            total = inbox[line, 0, here, :].astype(jnp.float32)
+            for part in range(1, n_split):
+                total = total + inbox[line, part, here, :].astype(jnp.float32)
+            squares = squares + jnp.sum(total * total, axis=1, keepdims=True)
+            sums.append(total)
+        scale = lax.rsqrt(squares / full + 1e-06) / math.sqrt(full)
+        for line in range(n_line):
+            unit_ref[here, line * wide : (line + 1) * wide] = (sums[line] * scale).astype(jnp.bfloat16)
+
+    for i in range(1, n_gen):
+        peer = lax.rem(g + i, n_gen)
+        landed(metas_ref.at[peer], meta_recv.at[peer])
+        meta_copy(i).wait_send()
+    for line in range(n_line):
+        side(shard(line, x), line).wait_send()
+
+        @pl.when((z < n_line - 1) & (line <= z))
+        def _():
+            up(shard(line, x), line).wait_send()
+
+        @pl.when((z > 0) & (line >= z))
+        def _():
+            down(shard(line, x), line).wait_send()
+
+        for i in range(1, n_split):
+            term_copy(line, lax.rem(s + i, n_split)).wait_send()
+
+
+def project(hidden, w_proj, meta, n_gen, n_split):
+    h = hidden.reshape(hidden.shape[0] * hidden.shape[1], hidden.shape[2])
+    depth, width = w_proj.shape
+    n_line = n_gen // PAIR
+    rows = h.shape[0] // n_split
+    wide = PAIR * width
+    dma = pltpu.SemaphoreType.DMA
+    vmem = pl.BlockSpec(memory_space=pltpu.VMEM)
+    return pl.pallas_call(
+        functools.partial(project_kernel, n_gen, n_split),
+        out_shape=(
+            jax.ShapeDtypeStruct((rows, n_gen * width), jnp.bfloat16),
+            jax.ShapeDtypeStruct((n_gen,) + meta.shape, jnp.float32),
+        ),
+        in_specs=[pl.BlockSpec(memory_space=pl.ANY), vmem, vmem],
+        out_specs=(vmem, vmem),
+        scratch_shapes=[
+            pltpu.VMEM(h.shape, jnp.bfloat16),
+            pltpu.VMEM((n_line, depth, wide), jnp.bfloat16),
+            pltpu.VMEM((n_line, n_split, rows, wide), jnp.bfloat16),
+            pltpu.VMEM((n_line, n_split, rows, wide), jnp.bfloat16),
+            dma, dma((n_line,)), dma((n_line,)), dma((n_line,)), dma((n_line,)), dma((n_line,)),
+            dma((n_line, n_split)), dma((n_line, n_split)), dma((n_gen,)), dma((n_gen,)),
+        ],
+        compiler_params=pltpu.CompilerParams(
+            collective_id=0, has_side_effects=True, vmem_limit_bytes=40 * 1024 * 1024
+        ),
+        cost_estimate=pl.CostEstimate(
+            flops=2 * h.shape[0] * depth * n_gen * width, bytes_accessed=h.size * 2, transcendentals=0
+        ),
+    )(h, w_proj, meta)
 
 
 def column_best(row_flat, gathered, member_len):
@@ -22,11 +240,7 @@
     return jnp.max(scores, axis=2)
 
 
-def body(hidden, w_proj, slot_prompt, lengths, weights, owner):
-    n_gen = lax.axis_size("gen")
-    n_split = lax.axis_size("split")
-    seq_part = hidden.shape[0] // n_split
-    slots = hidden.shape[1]
+def unit_plain(hidden, w_proj):
     w_block = lax.all_gather(w_proj, "gen", axis=1, tiled=True)
     emb_width = w_block.shape[1]
     projected = lax.psum_scatter(
@@ -41,6 +255,21 @@
         emb_width
     )
     unit = (projected * scale).astype(jnp.bfloat16)
+    return unit
+
+
+def body(hidden, w_proj, slot_prompt, lengths, weights, owner):
+    n_gen = lax.axis_size("gen")
+    n_split = lax.axis_size("split")
+    seq_part = hidden.shape[0] // n_split
+    slots = hidden.shape[1]
+    emb_width = w_proj.shape[1] * n_gen
+    if w_proj.shape[1] % 128 == 0 and n_gen % PAIR == 0:
+        meta = jnp.zeros((8, 128), jnp.float32)
+        unit, metas = project(hidden, w_proj, meta, n_gen, n_split)
+        unit = unit.reshape(seq_part, slots, emb_width)
+    else:
+        unit = unit_plain(hidden, w_proj)
     owner_cap = (MAXS + n_gen - 1) // n_gen
     buffer_slots = n_gen * owner_cap
     owner_hit = slot_prompt[:, None] == jnp.arange(n_gen, dtype=jnp.int32)[None, :]

time: 229 us -> 173 us (0.76)
  waiting for transfers between devices: 128 us -> 20.2 us
  Pallas kernels: 0 us -> 58 us
  matrix products: 17.6 us -> 8.23 us
  local copies, waits for them, and re-layouts: 12.6 us -> 15.8 us
    all_gather x1 -> x0, waiting for transfers between devices: 76.3 us -> none  [body(): w_block = lax.all_gather(w_proj, 'gen', axis=1, tiled=True)]
    pallas_call x0 -> x1, Pallas kernels: none -> 58 us  [project(): pl.pallas_call(functools.partial(project_kernel, n_gen, n_split), out_sha...]
    reduce_scatter x1 -> x0, waiting for transfers between devices: 30.2 us -> none  [body(): lax.psum_scatter(jnp.einsum('psh,he->pse', hidden, w_block, preferred_ele...]
    dot_general x1 -> x0, matrix products: 9.28 us -> none  [body(): jnp.einsum('psh,he->pse', hidden, w_block, preferred_element_type=jnp.flo...]
    unnamed x8, local copies, waits for them, and re-layouts: 0.02 us -> 3.23 us
  transfers between devices with their start and end apart: 4 -> 2, of which waited for: 4 -> 2; matrix products, arithmetic and copies ran while one was open for 4% -> 5% of each run, Pallas kernels for 0% -> 0%
where the time goes in v1:
time: 173 us; the launch traced here: 170 us
  Pallas kernels  58 us (34%)
  blocking collectives  39.4 us (23%)
  waiting for transfers between devices  20.2 us (12%)
  local copies, waits for them, and re-layouts  15.8 us (9%)
  between operations  13.6 us (8%)
  other arithmetic  9.11 us (5%)
  matrix products  8.23 us (5%)
  starting transfers between devices  5.92 us (3%)
    pallas_call x1, Pallas kernels, project(): pl.pallas_call(functools.partial(project_kernel, n_gen, n_split), out_sha...  58 us
    all_to_all x1, blocking collectives, body(): lax.all_to_all(send_unit, 'gen', split_axis=1, concat_axis=1, tiled=True)  29.2 us
    all_gather x1, waiting for transfers between devices, body(): every = lax.all_gather(arrived, 'split', axis=0, tiled=True)  17.9 us
    psum x1, blocking collectives, body(): summed = lax.psum(partial_sums, 'split')  10.2 us
    dot_general x1, matrix products, column_best(): lax.dot_general(row_flat, col_flat, (((1,), (1,)), ((), ())), preferred_e...  8.23 us
    all_to_all x1, starting transfers between devices, body(): lax.all_to_all(send_meta, 'gen', split_axis=1, concat_axis=1, tiled=True)  5.92 us
    gather x1, local copies, waits for them, and re-layouts, body(): columns = jnp.take(every, position, axis=1)  4.97 us
  transfers between devices with their start and end apart: 2, of which 2 were waited for; matrix products, arithmetic and copies ran while one was open for 5% of the time, Pallas kernels for 0%

profile of v1, /device:TPU:29, one launch (start us, length us, event | category | flops | bytes accessed | tf_op | source)
XLA Modules:
  0.0 170.3 jit_solution(5036954372498313234)
XLA Ops:
  6.5 0.0 copy-start
  6.5 0.0 all-gather.2.cloned.1.call-start
  6.5 0.9 convert_reduce_fusion.2
  7.4 0.8 select_reduce_fusion.3
  8.2 0.1 select_reduce_fusion.2
  8.4 0.0 copy-start.1
  8.4 2.2 %copy-done.1 = bf16[32,32,2048]{2,1,0:T(8,128)(2,1)S(1)} copy-done((bf16[32,32,2048]{2,1,0:T(8,128)(2,1)S(1)}, bf16[32,32,2048]{2,1,0:T(8,128)(2,1)}, u32[]{:S(2)}) %copy-start.1) | copy-done | bytes 4194328
  10.5 1.0 copy-done.2
  11.6 58.0 %shard_map.64 = (bf16[256,1024]{1,0:T(8,128)(2,1)S(1)}, f32[8,8,128]{2,1,0:T(8,128)}) custom-call(bf16[1024,2048]{1,0:T(8,128)(2,1)S(1)} %bitcast.34, bf16[2048,128]{1,0:T(8,128)(2,1)S(1)} %copy-done.2, f32[8,128]{1,0:T(8,128)S(1)} %broadcast_in_dim.150.meta_ref), custom_call_target="tpu_custom_call" | custom-call | flops 4294967296 | bytes 4194304 | tf_op jit(solution)/shard_map/pallas_call | solution.py:204
  69.6 0.3 copy.24
  69.9 0.0 copy-start.3
  69.9 0.6 gather_fusion.3
  70.6 0.2 select_bitcast_fusion.2
  70.7 29.2 %all_to_all.11 = bf16[8,64,1024]{2,0,1:T(8,128)(2,1)} all-to-all(bf16[8,64,1024]{2,0,1:T(8,128)(2,1)S(1)} %select_bitcast_fusion.2), channel_id=1, replica_groups=mesh['gen'=8,'split'=4] {'gen'}, dimensions={1} | all-to-all | bytes 2097152 | tf_op jit(solution)/shard_map/all_to_all | solution.py:290
  100.0 0.0 all-gather.2.cloned.1.call-update
  100.0 0.1 reduce_sum.80
  100.1 0.8 gather_fusion
  100.9 0.1 gather.33
  101.0 0.1 gt.47
  101.1 0.8 gather_fusion.1
  101.8 0.1 gather.35
  102.0 0.6 copy.21
  102.6 5.9 %all-to-all-start = ((bf16[2,8,8]{2,0,1:T(2,128)(2,1)}), bf16[2,8,8]{2,0,1:T(2,128)(2,1)S(1)}, u32[]{:S(2)}, u32[]{:S(2)}) async-start(bf16[2,8,8]{2,0,1:T(2,128)(2,1)} %copy.21), calls=%async_computation | async-start | bytes 8192 | tf_op jit(solution)/shard_map/all_to_all | solution.py:291
  108.5 2.3 %all-to-all-done = bf16[2,8,8]{2,0,1:T(2,128)(2,1)S(1)} async-done(((bf16[2,8,8]{2,0,1:T(2,128)(2,1)}), bf16[2,8,8]{2,0,1:T(2,128)(2,1)S(1)}, u32[]{:S(2)}, u32[]{:S(2)}) %all-to-all-start) | async-done | bytes 288 | tf_op jit(solution)/shard_map/all_to_all | solution.py:291
  110.8 0.1 reshape.390
  110.9 0.1 reduce-window.4
  111.0 0.1 reduce
  111.1 0.5 slice.30
  111.6 0.1 reshape.331
  111.7 0.1 reshape.330
  111.8 0.1 convert_reduce_fusion
  111.9 0.8 gather_fusion.6
  112.7 0.8 gather_fusion.2
  113.5 1.2 fusion.12
  114.7 0.6 maximum_convert_fusion
  115.3 0.1 broadcast_compare_fusion
  115.3 1.8 %gather_fusion.4 = bf16[64,8,1024]{2,1,0:T(8,128)(2,1)S(1)} fusion(bf16[8,64,1024]{2,0,1:T(8,128)(2,1)} %all_to_all.11, s32[1024]{0:T(1024)S(1)} %pad_clamp_fusion), kind=kCustom, calls=%fused_computation.4 | custom fusion | bytes 2097408 | tf_op jit(solution)/shard_map/jit(_take)/gather | solution.py:302
  117.2 0.2 select_bitcast_fusion.1
  117.4 17.9 %all-gather.2.cloned.1.call-done = bf16[32,64,1024]{2,0,1:T(8,128)(2,1)} async-done(((bf16[8,64,1024]{2,0,1:T(8,128)(2,1)}), bf16[32,64,1024]{2,0,1:T(8,128)(2,1)}) %all-gather.2.cloned.1.call-update) | async-done | bytes 4194320 | tf_op jit(solution)/shard_map/all_gather | solution.py:304
  135.3 5.0 %gather_fusion.5 = bf16[64,32,1024]{2,1,0:T(8,128)(2,1)} fusion(bf16[32,64,1024]{2,0,1:T(8,128)(2,1)} %all-gather.2.cloned.1.call-done, s32[1024]{0:T(1024)S(1)} %pad_clamp_fusion), kind=kCustom, calls=%fused_computation.5 | custom fusion | bytes 8388864 | tf_op jit(solution)/shard_map/jit(_take)/gather | solution.py:305
  140.2 2.6 %select_bitcast_fusion = bf16[32,64,1024]{2,0,1:T(8,128)(2,1)S(1)} fusion(bf16[64,32,1024]{2,1,0:T(8,128)(2,1)} %gather_fusion.5, pred[64]{0:T(512)(128)(4,1)S(1)} %get-tuple-element.11), kind=kLoop, calls=%fused_computation.11 | loop fusion | flops 2097152 | bytes 8388672 | tf_op jit(solution)/shard_map/jit(_take)/select_n | solution.py:305
  142.9 8.2 %select_reduce_fusion = f32[8,64,64]{2,1,0:T(8,128)S(1)} fusion(pred[32,64]{1,0:T(8,128)(4,1)S(1)} %iota_compare_fusion.1, bf16[32,64,1024]{2,0,1:T(8,128)(2,1)S(1)} %select_bitcast_fusion, bf16[8,64,1024,1]{2,0,1,3:T(8,128)(2,1)S(1)} %select_bitcast_fusion.1), kind=kOutput, calls=%fused_computation.7 | convolution fusion | flops 2149548032 | bytes 5376000 | tf_op jit(solution)/shard_map/dot_general | solution.py:233
  151.1 0.1 select_reduce_fusion.1
  151.2 10.2 %psum.7 = f32[64,64]{1,0:T(8,128)S(1)} all-reduce(f32[64,64]{1,0:T(8,128)S(1)} %select_reduce_fusion.1), channel_id=1, replica_groups=mesh['gen'=8,'split'=4] {'split'}, use_global_device_ids=true, to_apply=%region_8.9 | all-reduce | flops 4096 | bytes 32768 | tf_op jit(solution)/shard_map/psum | solution.py:310
  161.4 0.1 broadcast_divide_fusion
  161.5 0.1 copy.27
  161.6 0.2 fusion.7
  161.8 1.7 %compare_select_fusion.5 = f32[1,64]{1,0:T(1,128)} fusion(f32[64]{0:T(128)S(1)} %fusion.7, f32[]{:T(128)} %get-tuple-element.9, s32[]{:T(128)} %bitcast.2), kind=kLoop, calls=%fused_computation.49 | loop fusion | flops 192 | bytes 520 | tf_op jit(solution)/shard_map/jit(_where)/select_n | solution.py:314
  (20 shorter events, 0.1 us)
Async XLA Ops:
  6.5 93.6 %copy-start = (s32[32]{0:T(128)S(1)}, s32[32]{0:T(128)}, u32[]{:S(2)}) copy-start(s32[32]{0:T(128)} %param.9) | copy-start | bytes 388
  6.5 128.7 %all-gather.2.cloned.1.call-start = ((), (), s32[]{:S(2)}) async-start(), calls=%async_computation.2 | async-start | bytes 5242880 | tf_op jit(solution)/shard_map/all_gather | solution.py:304
  8.4 2.2 %copy-start.1 = (bf16[32,32,2048]{2,1,0:T(8,128)(2,1)S(1)}, bf16[32,32,2048]{2,1,0:T(8,128)(2,1)}, u32[]{:S(2)}) copy-start(bf16[32,32,2048]{2,1,0:T(8,128)(2,1)} %param.6) | copy-start | bytes 12582916
  10.5 1.0 copy-start.2
  69.9 31.1 %copy-start.3 = (bf16[32]{0:T(256)(128)(2,1)S(1)}, bf16[32]{0:T(256)(128)(2,1)}, u32[]{:S(2)}) copy-start(bf16[32]{0:T(256)(128)(2,1)} %param.10) | copy-start | bytes 196
  102.6 8.3 %all-to-all-start = ((bf16[2,8,8]{2,0,1:T(2,128)(2,1)}), bf16[2,8,8]{2,0,1:T(2,128)(2,1)S(1)}, u32[]{:S(2)}, u32[]{:S(2)}) async-start(bf16[2,8,8]{2,0,1:T(2,128)(2,1)} %copy.21), calls=%async_computation | async-start | bytes 8192 | tf_op jit(solution)/shard_map/all_to_all | solution.py:291
Sparse Core Ops, SparseCore 0:
  100.1 35.0 all-gather.1

commit v2 on v1

--- a/solution.py
+++ b/solution.py
@@ -226,6 +226,181 @@
     )(h, w_proj, meta)
 
 
+def match_kernel(
+    n_gen, n_split, cap, unit_ref, sel_ref, len_ref, mask_ref, out_ref, staging, held, sums,
+    send_sem, recv_sem, far_send, far_recv, near_send, near_recv, sum_send, sum_recv,
+):
+    g = lax.axis_index("gen")
+    s = lax.axis_index("split")
+    far = lax.rem(s + 2, n_split)
+    near = s + 1 - 2 * lax.rem(s, 2)
+    near_far = lax.rem(near + 2, n_split)
+    block = staging.shape[1]
+    positions = block // cap
+    greet(n_gen, n_split)
+
+    def landed(ref, sem):
+        pltpu.make_async_copy(ref, ref, sem).wait()
+
+    def deliver(i):
+        peer = lax.rem(g + i, n_gen)
+        return pltpu.make_async_remote_copy(
+            src_ref=staging.at[peer], dst_ref=held.at[s, g], send_sem=send_sem.at[peer],
+            recv_sem=recv_sem.at[g], device_id={"gen": peer}, device_id_type=MESH,
+        )
+
+    def share(part, source, to, out_sem, in_sem):
+        return pltpu.make_async_remote_copy(
+            src_ref=held.at[part, source], dst_ref=held.at[part, source], send_sem=out_sem,
+            recv_sem=in_sem, device_id={"split": to}, device_id_type=MESH,
+        )
+
+    def to_far(source):
+        return share(s, source, far, far_send.at[source], far_recv.at[source])
+
+    def to_near(source):
+        return share(s, source, near, near_send.at[0, source], near_recv.at[0, source])
+
+    def relay(source):
+        return share(far, source, near, near_send.at[1, source], near_recv.at[1, source])
+
+    def stage(peer):
+        return jnp.dot(
+            sel_ref[peer], unit_ref[...], preferred_element_type=jnp.float32
+        ).astype(jnp.bfloat16)
+
+    for i in range(1, n_gen):
+        peer = lax.rem(g + i, n_gen)
+        staging[peer] = stage(peer)
+        deliver(i).start()
+    held[s, g] = stage(g)
+    to_far(g).start()
+    to_near(g).start()
+    for i in range(1, n_gen + 1):
+        if i < n_gen:
+            source = lax.rem(g + n_gen - i, n_gen)
+            landed(held.at[s, source], recv_sem.at[source])
+            to_far(source).start()
+            to_near(source).start()
+        before = lax.rem(g + n_gen - (i - 1), n_gen)
+        landed(held.at[far, before], far_recv.at[before])
+        relay(before).start()
+
+    full = held.shape[3]
+    rows = held[s].reshape(n_gen * block, full)
+    lens = len_ref[...].reshape(n_gen, 1, cap, 1)
+
+    def part_best(part):
+        sim = lax.dot_general(
+            held[part].reshape(n_gen * block, full), rows, (((1,), (1,)), ((), ())),
+            preferred_element_type=jnp.float32,
+        ).reshape(n_gen, positions, cap, n_gen * block)
+        at = part * positions + lax.broadcasted_iota(jnp.int32, (n_gen, positions, cap, 1), 1)
+        return jnp.max(jnp.where(at < lens, sim, jnp.float32(-2.0)), axis=1)
+
+    best = jnp.maximum(part_best(s), part_best(far))
+    for source in range(n_gen):
+        landed(held.at[near, source], near_recv.at[0, source])
+    best = jnp.maximum(best, part_best(near))
+    for source in range(n_gen):
+        landed(held.at[near_far, source], near_recv.at[1, source])
+    best = jnp.maximum(best, part_best(near_far))
+    sums[s] = jnp.dot(
+        best.reshape(n_gen * cap, n_gen * block), mask_ref[...],
+        preferred_element_type=jnp.float32, precision=lax.Precision.HIGHEST,
+    )
+
+    def sum_copy(i):
+        peer = lax.rem(s + i, n_split)
+        return pltpu.make_async_remote_copy(
+            src_ref=sums.at[s], dst_ref=sums.at[s], send_sem=sum_send.at[peer],
+            recv_sem=sum_recv.at[s], device_id={"split": peer}, device_id_type=MESH,
+        )
+
+    for i in range(1, n_split):
+        sum_copy(i).start()
+    for i in range(1, n_split):
+        peer = lax.rem(s + i, n_split)
+        landed(sums.at[peer], sum_recv.at[peer])
+    total = sums[0]
+    for part in range(1, n_split):
+        total = total + sums[part]
+    out_ref[...] = total
+    for i in range(1, n_split):
+        sum_copy(i).wait_send()
+    for i in range(1, n_gen):
+        deliver(i).wait_send()
+    for source in range(n_gen):
+        to_far(source).wait_send()
+        to_near(source).wait_send()
+        relay(source).wait_send()
+
+
+def match(unit, sel, member_len, mask, n_gen, n_split, cap):
+    block, full = sel.shape[1], unit.shape[1]
+    dma = pltpu.SemaphoreType.DMA
+    vmem = pl.BlockSpec(memory_space=pltpu.VMEM)
+    return pl.pallas_call(
+        functools.partial(match_kernel, n_gen, n_split, cap),
+        out_shape=jax.ShapeDtypeStruct((n_gen * cap, 128), jnp.float32),
+        in_specs=[vmem] * 4,
+        out_specs=vmem,
+        scratch_shapes=[
+            pltpu.VMEM((n_gen, block, full), jnp.bfloat16),
+            pltpu.VMEM((n_split, n_gen, block, full), jnp.bfloat16),
+            pltpu.VMEM((n_split, n_gen * cap, 128), jnp.float32),
+            dma((n_gen,)), dma((n_gen,)), dma((n_gen,)), dma((n_gen,)), dma((2, n_gen)),
+            dma((2, n_gen)), dma((n_split,)), dma((n_split,)),
+        ],
+        compiler_params=pltpu.CompilerParams(
+            collective_id=1, has_side_effects=True, vmem_limit_bytes=40 * 1024 * 1024
+        ),
+    )(unit, sel, member_len, mask)
+
+
+def fused(hidden, w_proj, slot_prompt, lengths, weights, owner):
+    n_gen = lax.axis_size("gen")
+    n_split = lax.axis_size("split")
+    slots = hidden.shape[1]
+    positions = hidden.shape[0] // n_split
+    cap = MAXS // n_gen
+    f32 = jnp.float32
+    meta = jnp.stack([slot_prompt.astype(f32), lengths.astype(f32), weights.astype(f32)])
+    meta = jnp.pad(meta, ((0, 5), (0, 128 - slots)))
+    unit, metas = project(hidden, w_proj, meta, n_gen, n_split)
+    ids = jnp.arange(n_gen, dtype=jnp.int32)
+    dest = jnp.sum(jnp.where(slot_prompt[:, None] == ids[None, :], owner[None, :], 0), axis=1)
+    local = jnp.arange(slots, dtype=jnp.int32)
+    same = (slot_prompt[:, None] == slot_prompt[None, :]) & (local[:, None] > local[None, :])
+    key = dest * cap + jnp.sum(same.astype(jnp.int32), axis=1)
+    place = jnp.arange(positions, dtype=jnp.int32)
+    lane = jnp.arange(cap, dtype=jnp.int32)
+    sel = (key[None, None, None, None, :] == (ids[:, None] * cap + lane)[:, None, :, None, None]) & (
+        place[None, :, None, None, None] == place[None, None, None, :, None]
+    )
+    sel = sel.astype(jnp.bfloat16).reshape(n_gen, positions * cap, positions * slots)
+    mine = jnp.sum(jnp.where(owner == lax.axis_index("gen"), ids, 0))
+    hit = metas[:, 0, :slots] == mine.astype(f32)
+    rank = jnp.sum((hit[:, None, :] & (local[:, None] > local[None, :])[None]).astype(jnp.int32), axis=2)
+    pick = hit[:, None, :] & (rank[:, None, :] == lane[None, :, None])
+    member_len = jnp.sum(jnp.where(pick, metas[:, None, 1, :slots], 0.0), axis=2).reshape(MAXS).astype(jnp.int32)
+    member_weight = jnp.sum(jnp.where(pick, metas[:, None, 2, :slots], 0.0), axis=2).reshape(MAXS)
+    member = (ids[:, None, None] * cap + lane + 0 * place[:, None]).reshape(-1)
+    time = lax.axis_index("split") * positions + (place[:, None] + 0 * ids[:, None, None] + 0 * lane).reshape(-1)
+    column = jnp.arange(128, dtype=jnp.int32)
+    wide_len = jnp.pad(member_len, (0, 128 - MAXS))
+    mask = ((member[:, None] == column[None, :]) & (time[:, None] < wide_len[None, :])).astype(f32)
+    summed = match(unit, sel, member_len[:, None], mask, n_gen, n_split, cap)[:, :MAXS]
+    recall = summed / jnp.maximum(member_len, 1).astype(f32)[None, :]
+    score = 0.5 * (recall + recall.T)
+    util = jnp.sum(score * member_weight[None, :], axis=1) / jnp.sum(member_weight)
+    live = member_len > 0
+    order = jnp.arange(MAXS, dtype=jnp.int32)
+    spot = jnp.sum((live[None, :] & (order[None, :] < order[:, None])).astype(jnp.int32), axis=1)
+    chosen = live[None, :] & (spot[None, :] == order[:, None])
+    return jnp.sum(jnp.where(chosen, util[None, :], 0.0), axis=1)[None, :]
+
+
 def column_best(row_flat, gathered, member_len):
     amount = gathered.shape[0]
     slots_here = gathered.shape[1]
@@ -263,13 +438,8 @@
     n_split = lax.axis_size("split")
     seq_part = hidden.shape[0] // n_split
     slots = hidden.shape[1]
-    emb_width = w_proj.shape[1] * n_gen
-    if w_proj.shape[1] % 128 == 0 and n_gen % PAIR == 0:
-        meta = jnp.zeros((8, 128), jnp.float32)
-        unit, metas = project(hidden, w_proj, meta, n_gen, n_split)
-        unit = unit.reshape(seq_part, slots, emb_width)
-    else:
-        unit = unit_plain(hidden, w_proj)
+    unit = unit_plain(hidden, w_proj)
+    emb_width = unit.shape[2]
     owner_cap = (MAXS + n_gen - 1) // n_gen
     buffer_slots = n_gen * owner_cap
     owner_hit = slot_prompt[:, None] == jnp.arange(n_gen, dtype=jnp.int32)[None, :]
@@ -316,7 +486,9 @@
 
 
 def solution(mesh):
+    n_gen, n_split = mesh.shape["gen"], mesh.shape["split"]
+    narrow = n_gen % PAIR == 0 and MAXS % n_gen == 0 and n_gen <= 8 and n_split == 4
     placed = (P(None, "gen", "split"), P("split", "gen"), P("gen"), P("gen"), P("gen"), P())
     return jax.shard_map(
-        body, mesh=mesh, in_specs=placed, out_specs=P("gen", None), check_vma=False
-    )
+        fused if narrow else body, mesh=mesh, in_specs=placed, out_specs=P("gen", None), check_vma=False
+    )

time: 173 us -> 118 us (0.68); the launches traced: 170 us -> 118 us
  Pallas kernels: 58 us -> 105 us
  blocking collectives: 39.4 us -> 0 us
  waiting for transfers between devices: 20.2 us -> 0 us
  between operations: 13.6 us -> 0.82 us
  local copies, waits for them, and re-layouts: 15.8 us -> 4.89 us
  matrix products: 8.23 us -> 0 us
  starting transfers between devices: 5.92 us -> 0 us
  other arithmetic: 9.11 us -> 7.14 us
    pallas_call x0 -> x1, Pallas kernels: none -> 47.5 us  [match(): pl.pallas_call(functools.partial(match_kernel, n_gen, n_split, cap), out_...]
    all_to_all x1 -> x0, blocking collectives: 29.2 us -> none  [body(): lax.all_to_all(send_unit, 'gen', split_axis=1, concat_axis=1, tiled=True)]
    all_gather x1 -> x0, waiting for transfers between devices: 17.9 us -> none  [body(): every = lax.all_gather(arrived, 'split', axis=0, tiled=True)]
    gather x9 -> x0, local copies, waits for them, and re-layouts: 10.7 us -> none  [the longest x1 4.97 us: body(): columns = jnp.take(every, position, axis=1)]
    psum x1 -> x0, blocking collectives: 10.2 us -> none  [body(): summed = lax.psum(partial_sums, 'split')]
    dot_general x1 -> x0, matrix products: 8.23 us -> none  [column_best(): lax.dot_general(row_flat, col_flat, (((1,), (1,)), ((), ())), preferred_e...]
    all_to_all x1 -> x0, starting transfers between devices: 5.92 us -> none  [body(): lax.all_to_all(send_meta, 'gen', split_axis=1, concat_axis=1, tiled=True)]
    select_n x7 -> x0, other arithmetic: 4.69 us -> none  [the longest x1 2.62 us: body(): columns = jnp.take(every, position, axis=1)]
  transfers between devices with their start and end apart: 2 -> 0, of which waited for: 2 -> 0; matrix products, arithmetic and copies ran while one was open for 5% -> 0% of each run, Pallas kernels for 0% -> 0%
where the time goes in v2:
time: 118 us
  Pallas kernels  105 us (89%)
  other arithmetic  7.14 us (6%)
  local copies, waits for them, and re-layouts  4.89 us (4%)
    pallas_call x1, Pallas kernels, project(): pl.pallas_call(functools.partial(project_kernel, n_gen, n_split), out_sha...  57.4 us
    pallas_call x1, Pallas kernels, match(): pl.pallas_call(functools.partial(match_kernel, n_gen, n_split, cap), out_...  47.5 us
    unnamed x5, local copies, waits for them, and re-layouts  3.23 us

profile of v2, /device:TPU:29, one launch (start us, length us, event | category | flops | bytes accessed | tf_op | source)
XLA Modules:
  0.0 117.8 jit_solution(14798062989719957214)
XLA Ops:
  0.0 1.3 %fusion.7 = s32[]{:T(128)} fusion(s32[8]{0:T(128)} %param.11, s32[]{:T(128)S(6)} %axis_index.23), kind=kLoop, calls=%fused_computation.36 | loop fusion | flops 23 | bytes 40 | tf_op jit(solution)/shard_map/reduce_sum | solution.py:382
  1.9 0.7 bitcast_convert_fusion
  2.6 0.8 select_reduce_fusion.4
  3.4 0.9 convert_reduce_fusion.2
  4.3 0.7 convert_bitcast_fusion
  5.0 0.1 iota_add_fusion.1
  5.1 0.1 broadcast_compare_fusion
  5.2 0.1 eq.135
  5.3 0.1 add.74
  5.4 0.1 and.77
  5.4 0.2 and.78
  5.6 0.2 and.75
  5.8 0.8 and.76
  6.5 0.1 and_convert_fusion.sel_ref
  6.6 0.0 copy-start
  6.6 2.2 %copy-done = bf16[32,32,2048]{2,1,0:T(8,128)(2,1)S(1)} copy-done((bf16[32,32,2048]{2,1,0:T(8,128)(2,1)S(1)}, bf16[32,32,2048]{2,1,0:T(8,128)(2,1)}, u32[]{:S(2)}) %copy-start) | copy-done | bytes 4194328
  8.8 0.0 copy-start.1
  8.8 1.0 copy-done.1
  9.8 57.4 %shard_map.64 = (bf16[256,1024]{1,0:T(8,128)(2,1)S(1)}, f32[8,8,128]{2,1,0:T(8,128)S(1)}) custom-call(bf16[1024,2048]{1,0:T(8,128)(2,1)S(1)} %bitcast.24, bf16[2048,128]{1,0:T(8,128)(2,1)S(1)} %copy-done.1, f32[8,128]{1,0:T(8,128)S(1)} %select_maximum_fusion.meta_ref), custom_call_target="tpu_custom_call" | custom-call | flops 4294967296 | bytes 4194304 | tf_op jit(solution)/shard_map/pallas_call | solution.py:204
  67.3 0.2 convert_reduce_fusion
  67.6 0.6 select_reduce_fusion
  68.2 0.1 mul.51
  68.3 0.1 convert_element_type.63
  68.4 0.1 convert_reduce_fusion.1
  68.5 0.1 convert_element_type.70.len_ref
  68.6 0.2 fusion.1.mask_ref
  68.8 47.5 %shard_map.65 = f32[64,128]{1,0:T(8,128)S(1)} custom-call(bf16[256,1024]{1,0:T(8,128)(2,1)S(1)} %get-tuple-element.8.unit_ref, bf16[8,64,256]{2,1,0:T(8,128)(2,1)S(1)} %and_convert_fusion.sel_ref, s32[64,1]{1,0:T(8,128)S(1)} %convert_element_type.70.len_ref, f32[512,128]{1,0:T(8,128)S(1)} %fusion.1.mask_ref), custom_call_target="tpu_custom_call" | custom-call | tf_op jit(solution)/shard_map/pallas_call | solution.py:343
  116.3 0.1 copy.12
  116.3 0.1 fusion.3
  116.5 0.7 broadcast_divide_fusion
  117.1 0.6 select_reduce_fusion.2
  (16 shorter events, 0.1 us)
Async XLA Ops:
  6.6 2.2 %copy-start = (bf16[32,32,2048]{2,1,0:T(8,128)(2,1)S(1)}, bf16[32,32,2048]{2,1,0:T(8,128)(2,1)}, u32[]{:S(2)}) copy-start(bf16[32,32,2048]{2,1,0:T(8,128)(2,1)} %param.6) | copy-start | bytes 12582916
  8.8 1.0 copy-start.1
